TPU v7x, 256 devices: a whole 4x4x8 slice. The times are simulated.
256 devices in a mesh: dp: 8 (over z_hi, core), row: 16 (over y, x), col: 2 (over z_lo).
Axes of the slice: x: 4, y: 4, z: 8 (z_hi: 4, z_lo: 2; z = z_hi * 2 + z_lo), core: 2. Of those that a mesh axis runs over, the one named last changes fastest.
Arguments:
- hidden_pre: bfloat16 [12288, 12288], P(('dp', 'col'), 'row'), may hold values from -8 to 8
- out_grad: bfloat16 [12288, 6144], P(('dp', 'row'), 'col'), may hold values from -6 to 6
- down_weight: bfloat16 [12288, 6144], P('row', 'col'), may hold values from -0.0546875 to 0.0546875
- tile_mask: int32 [96, 48], P('row', 'col'), may hold values from 0 to 1, as said below
Outputs:
- in_grad: bfloat16 [12288, 12288], P(('dp', 'col'), 'row')
- weight_grad: bfloat16 [12288, 6144], P(('row', 'dp'), 'col')
Inputs may be any that keep to these rules, and one draw needn't show every extreme that they name: Each row of tile_mask holds exactly 24 ones; which tile columns are kept, and so how many fall on each device, varies.
All inputs are finite; a program needn't handle non-finite values.
Results may differ from a plain program's by a relative error of at most 0.017.
Values may be sent and summed in bfloat16 or wider, within the bound.
A program may use at most 128 MiB of HBM per device.

v0:
```python
import math

import jax
import jax.numpy as jnp
from jax import lax
from jax.sharding import PartitionSpec as P


def gelu_slope(values):
    normal_cdf = 0.5 * (1.0 + lax.erf(values * 0.7071067811865476))
    density = jnp.exp(-0.5 * values * values) * 0.3989422804014327
    return normal_cdf + values * density


def body(hidden_pre, out_grad, down_weight, tile_mask):
    tile_size = down_weight.shape[0] // tile_mask.shape[0]
    kept_mask = jnp.repeat(jnp.repeat(tile_mask, tile_size, axis=0), tile_size, axis=1).astype(
        jnp.bfloat16
    )
    masked = down_weight * kept_mask
    group_grads = lax.all_gather(out_grad, "row", axis=0, tiled=True)
    group_tokens = group_grads.shape[0]
    scaling = 1.0 / math.sqrt(group_tokens * lax.axis_size("dp"))
    own_rows = lax.all_to_all(group_grads, "col", split_axis=0, concat_axis=1, tiled=True)
    full_weight = lax.all_gather(masked, "col", axis=1, tiled=True)
    backward = lax.dot_general(
        own_rows, full_weight, (((1,), (1,)), ((), ())), preferred_element_type=jnp.float32
    )
    derivative = gelu_slope(hidden_pre.astype(jnp.float32))
    in_grad = (backward * derivative).astype(jnp.bfloat16)
    group_pre = lax.all_gather(hidden_pre, "col", axis=0, tiled=True)
    activated = jax.nn.gelu(group_pre.astype(jnp.float32), approximate=False).astype(jnp.bfloat16)
    product = lax.dot_general(
        activated, group_grads, (((0,), (0,)), ((), ())), preferred_element_type=jnp.float32
    )
    summed = lax.psum_scatter(
        (product * scaling * kept_mask.astype(jnp.float32)).astype(jnp.bfloat16),
        "dp",
        scatter_dimension=0,
        tiled=True,
    )
    return (in_grad, summed)


def solution(mesh):
    return jax.shard_map(
        body,
        mesh=mesh,
        in_specs=(
            P(("dp", "col"), "row"),
            P(("dp", "row"), "col"),
            P("row", "col"),
            P("row", "col"),
        ),
        out_specs=(P(("dp", "col"), "row"), P(("row", "dp"), "col")),
        check_vma=False,
    )
```

profile of v0, /device:TPU:1, one launch (start us, length us, event | category | flops | bytes accessed | tf_op | source)
XLA Modules:
  0.0 403.5 jit_solution(15481081504411613394)
XLA Ops:
  7.2 0.0 all-gather.6.cloned.1.call-start
  7.2 0.7 all-gather.6.cloned.1.call-update
  7.9 0.0 all-gather.8.cloned.1.call-start
  7.9 0.7 all-gather.8.cloned.1.call-update
  8.6 0.0 all-gather.4.cloned.1.call-start
  8.7 0.8 convert_element_type.29
  9.6 2.9 broadcast_in_dim.7
  12.5 2.1 copy-done
  14.6 2.7 bitcast_multiply_fusion
  17.3 0.0 all-gather.4.cloned.1.call-update
  17.4 77.6 %all-gather.6.cloned.1.call-done = bf16[1536,3072]{1,0:T(8,128)(2,1)} async-done(((bf16[96,3072]{1,0:T(8,128)(2,1)}), bf16[1536,3072]{1,0:T(8,128)(2,1)}) %all-gather.6.cloned.1.call-update) | async-done | bytes 9437200 | tf_op jit(solution)/shard_map/all_gather | solution.py:21
  95.0 7.4 %all-to-all-start = ((bf16[2,768,3072]{2,1,0:T(8,128)(2,1)}), bf16[2,768,3072]{2,1,0:T(8,128)(2,1)}, u32[]{:S(2)}, u32[]{:S(2)}) async-start(bf16[2,768,3072]{2,1,0:T(8,128)(2,1)} %bitcast.17), calls=%async_computation | async-start | bytes 18874368 | tf_op jit(solution)/shard_map/all_to_all | solution.py:24
  102.4 0.0 reduce-scatter.2.cloned.1.call-start
  102.4 61.0 %all-gather.8.cloned.1.call-done = bf16[1536,768]{1,0:T(8,128)(2,1)} async-done(((bf16[768,768]{1,0:T(8,128)(2,1)}), bf16[1536,768]{1,0:T(8,128)(2,1)}) %all-gather.8.cloned.1.call-update) | async-done | bytes 2359312 | tf_op jit(solution)/shard_map/all_gather | solution.py:31
  163.4 24.2 %multiply_convert_fusion = bf16[768,3072]{1,0:T(8,128)(2,1)} fusion(bf16[1536,3072]{1,0:T(8,128)(2,1)} %all-gather.6.cloned.1.call-done, bf16[96,8,24,128]{3,2,1,0:T(8,128)(2,1)} %bitcast.16, bf16[1536,768]{1,0:T(8,128)(2,1)} %all-gather.8.cloned.1.call-done), kind=kOutput, calls=%fused_computation | convolution fusion | flops 7335051264 | bytes 21233664 | tf_op jit(solution)/shard_map/dot_general | solution.py:33
  187.6 0.0 reduce-scatter.2.cloned.1.call-update
  187.7 1.4 copy-done.2
  189.0 0.6 copy.11
  189.7 83.9 %all-to-all-done = bf16[2,768,3072]{2,1,0:T(8,128)(2,1)} async-done(((bf16[2,768,3072]{2,1,0:T(8,128)(2,1)}), bf16[2,768,3072]{2,1,0:T(8,128)(2,1)}, u32[]{:S(2)}, u32[]{:S(2)}) %all-to-all-start) | async-done | bytes 9437216 | tf_op jit(solution)/shard_map/all_to_all | solution.py:24
  273.5 12.6 %copy.10 = bf16[768,2,3072]{0,2,1:T(8,128)(2,1)} copy(bf16[768,2,3072]{2,0,1:T(8,128)(2,1)} %bitcast.2) | data formatting | bytes 18874368 | tf_op jit(solution)/shard_map/all_to_all | solution.py:24
  286.2 46.8 %all-gather.4.cloned.1.call-done = bf16[768,6144]{1,0:T(8,128)(2,1)} async-done(((bf16[768,3072]{1,0:T(8,128)(2,1)}), bf16[768,6144]{1,0:T(8,128)(2,1)}) %all-gather.4.cloned.1.call-update) | async-done | bytes 9437200 | tf_op jit(solution)/shard_map/all_gather | solution.py:25
  333.0 13.2 %fusion.69 = bf16[768,768]{0,1:T(8,128)(2,1)S(1)} fusion(bf16[768,768]{0,1:T(8,128)(2,1)S(1)} %copy.11, bf16[768,6144]{1,0:T(8,128)(2,1)} %all-gather.4.cloned.1.call-done, bf16[768,6144]{0,1:T(8,128)(2,1)} %bitcast.18), kind=kOutput, calls=%fused_computation.77 | convolution fusion | flops 7254245376 | bytes 21233664 | tf_op jit(solution)/shard_map/dot_general | solution.py:26
  346.2 1.5 copy.12
  347.6 49.4 %reduce-scatter.2.cloned.1.call-done = bf16[96,3072]{1,0:T(8,128)(2,1)} async-done(((bf16[768,3072]{1,0:T(8,128)(2,1)}), bf16[96,3072]{1,0:T(8,128)(2,1)}) %reduce-scatter.2.cloned.1.call-update) | async-done | bytes 589840 | tf_op jit(solution)/shard_map/reduce_scatter | solution.py:36
  (5 shorter events, 0.0 us)
Async XLA Ops:
  7.2 87.8 %all-gather.6.cloned.1.call-start = ((), (), s32[]{:S(2)}) async-start(), calls=%async_computation.3 | async-start | bytes 10027008 | tf_op jit(solution)/shard_map/all_gather | solution.py:21
  7.9 155.5 %all-gather.8.cloned.1.call-start = ((), (), s32[]{:S(2)}) async-start(), calls=%async_computation.4 | async-start | bytes 3538944 | tf_op jit(solution)/shard_map/all_gather | solution.py:31
  8.6 324.3 %all-gather.4.cloned.1.call-start = ((), (), s32[]{:S(2)}) async-start(), calls=%async_computation.2 | async-start | bytes 14155776 | tf_op jit(solution)/shard_map/all_gather | solution.py:25
  8.7 5.9 %copy-start.1 = (bf16[768,3072]{1,0:T(8,128)(2,1)S(1)}, bf16[768,3072]{1,0:T(8,128)(2,1)}, u32[]{:S(2)}) copy-start(bf16[768,3072]{1,0:T(8,128)(2,1)} %param.6) | copy-start | bytes 14155780
  12.5 2.1 copy-start
  95.0 178.6 %all-to-all-start = ((bf16[2,768,3072]{2,1,0:T(8,128)(2,1)}), bf16[2,768,3072]{2,1,0:T(8,128)(2,1)}, u32[]{:S(2)}, u32[]{:S(2)}) async-start(bf16[2,768,3072]{2,1,0:T(8,128)(2,1)} %bitcast.17), calls=%async_computation | async-start | bytes 18874368 | tf_op jit(solution)/shard_map/all_to_all | solution.py:24
  102.4 294.6 %reduce-scatter.2.cloned.1.call-start = ((), (), s32[]{:S(2)}) async-start(), calls=%async_computation.5 | async-start | bytes 5308416 | tf_op jit(solution)/shard_map/reduce_scatter | solution.py:36
  187.6 1.4 copy-start.2
Sparse Core Ops, SparseCore 0:
  10.4 84.5 all-gather.5
  96.8 66.5 all-gather.7
  165.2 167.7 all-gather.3
  336.0 60.9 reduce-scatter.1
where the time goes:
time: 406 us; the launch traced here: 404 us
  waiting for transfers between devices  320 us (79%)
  matrix products  37.4 us (9%)
  local copies, waits for them, and re-layouts  21.1 us (5%)
  between operations  13.8 us (3%)
  starting transfers between devices  7.54 us (2%)
    all_to_all x1, waiting for transfers between devices, body(): lax.all_to_all(group_grads, 'col', split_axis=0, concat_axis=1, tiled=True)  83.9 us
    all_gather x1, waiting for transfers between devices, body(): group_grads = lax.all_gather(out_grad, 'row', axis=0, tiled=True)  77.6 us
    all_gather x1, waiting for transfers between devices, body(): group_pre = lax.all_gather(hidden_pre, 'col', axis=0, tiled=True)  61 us
    reduce_scatter x1, waiting for transfers between devices, body(): lax.psum_scatter((product * scaling * kept_mask.astype(jnp.float32)).asty...  49.4 us
    all_gather x1, waiting for transfers between devices, body(): full_weight = lax.all_gather(masked, 'col', axis=1, tiled=True)  46.8 us
    dot_general x1, matrix products, body(): lax.dot_general(activated, group_grads, (((0,), (0,)), ((), ())), preferr...  24.2 us
    dot_general x1, matrix products, body(): lax.dot_general(own_rows, full_weight, (((1,), (1,)), ((), ())), preferre...  13.2 us
    all_to_all x1, local copies, waits for them, and re-layouts, body(): lax.all_to_all(group_grads, 'col', split_axis=0, concat_axis=1, tiled=True)  12.6 us
  transfers between devices with their start and end apart: 5, of which 5 were waited for; matrix products, arithmetic and copies ran while one was open for 15% of the time, Pallas kernels for 0%

commit v1 on v0

v1 whole, which is shorter than its diff:
```python
import functools
import math

import jax
import jax.numpy as jnp
from jax import lax
from jax.experimental import pallas as pl
from jax.experimental.pallas import tpu as pltpu
from jax.sharding import PartitionSpec as P

MESH = pl.DeviceIdType.MESH
BF, F32 = jnp.bfloat16, jnp.float32
CHUNKS = 8
PAIRS = CHUNKS // 2
WIDTH = 384
GROUPS = 4
SLOTS = 24
PER = SLOTS // GROUPS
EARLY = 2


def kernel(
    scaling,
    hp_ref, og_ref, w_ref, mask_ref, place_ref,
    in_ref, out_ref,
    gath, weight, act_t, act, slope, acc, dense, kept, summed, fin,
    land1, land2, land3, land4, place_in, table, tables,
    p0s, p0r, p1s, p1r, p2s, p2r, wls, wzs, wzr, wcs, wcr, ms, mr, tsem, cs, cr, rs, rr,
):
    dp, row, col = lax.axis_index("dp"), lax.axis_index("row"), lax.axis_index("col")
    x, y, core, a = lax.rem(row, 4), row // 4, lax.rem(dp, 2), dp // 2
    z = a * 2 + col

    def chip(px, py, pz, pc):
        px, py, pz = lax.rem(px + 4, 4), lax.rem(py + 4, 4), lax.rem(pz + 8, 8)
        return ((pz // 2) * 2 + pc, py * 4 + px, lax.rem(pz, 2))

    xp, xm = chip(x + 1, y, z, core), chip(x - 1, y, z, core)
    yp, ym = chip(x, y + 1, z, core), chip(x, y - 1, z, core)
    zp, zm = chip(x, y, z + 1, core), chip(x, y, z - 1, core)
    pair = (dp, row, 1 - col)
    other = chip(x, y, z - 1 + 2 * col, core)
    twin = (a * 2 + 1 - core, row, col)
    swap = (dp, lax.rem(row + 8, 16), 1 - col)
    crosses = row // 8 != col
    up, down = lax.rem(x + 1, 4), lax.rem(x + 3, 4)
    yup, ydown = lax.rem(y + 1, 4), lax.rem(y + 3, 4)

    def send(src, dst, s, r, to):
        return pltpu.make_async_remote_copy(
            src_ref=src, dst_ref=dst, send_sem=s, recv_sem=r, device_id=to, device_id_type=MESH
        )

    def same(ref, s, r, to):
        return send(ref, ref, s, r, to)

    def cross(j):
        return send(
            og_ref.at[:, pl.ds(j * WIDTH, WIDTH)],
            gath.at[j, lax.rem(y + 2, 4), x],
            p0s.at[j], p0r.at[j], swap,
        )

    def first(j, forward):
        if not forward:
            mine = gath.at[j, y, x]
            ends = (xp, xm) if j % 2 == 0 else (yp, ym)
            return [same(mine, p1s.at[j, k], p1r.at[j, k], ends[k]) for k in range(2)]
        if j % 2 == 0:
            parts = (gath.at[j, y, down, pl.ds(0, 48)], gath.at[j, y, up, pl.ds(48, 48)])
            ends = (xp, xm)
        else:
            parts = (gath.at[j, ydown, x, pl.ds(0, 48)], gath.at[j, yup, x, pl.ds(48, 48)])
            ends = (yp, ym)
        return [same(parts[k], p1s.at[j, 2 + k], p1r.at[j, 2 + k], ends[k]) for k in range(2)]

    def second(j, forward):
        if j % 2 == 0:
            ends = (yp, ym)
            if forward:
                parts = (gath.at[j, ydown, pl.ds(0, 2)], gath.at[j, yup, pl.ds(2, 2)])
            else:
                parts = (gath.at[j, y], gath.at[j, y])
        else:
            ends = (xp, xm)
            if forward:
                parts = (gath.at[j, pl.ds(0, 2), down], gath.at[j, pl.ds(2, 2), up])
            else:
                parts = (gath.at[j, :, x], gath.at[j, :, x])
        f = 2 if forward else 0
        return [same(parts[k], p2s.at[j, f + k], p2r.at[j, f + k], ends[k]) for k in range(2)]

    def both(make, p, forward):
        return make(2 * p, forward) + make(2 * p + 1, forward)

    def start(copies):
        for c in copies:
            c.start()

    def arrive(copies):
        for c in copies:
            c.wait_recv()

    def left(copies):
        for c in copies:
            c.wait_send()

    def start_cross(p):
        @pl.when(crosses)
        def _():
            cross(2 * p).start()
            cross(2 * p + 1).start()

    def wait_cross(p):
        @pl.when(crosses)
        def _():
            cross(2 * p).wait_recv()
            cross(2 * p + 1).wait_recv()

    def w_push(half):
        return [
            same(
                weight.at[col, pl.ds(4 * half, 4), pl.ds(384 * core + 192 * k, 192)],
                wzs.at[half, k], wzr.at[half, k], (zp, zm)[k],
            )
            for k in range(2)
        ]

    def w_relay(half):
        return same(
            weight.at[1 - col, pl.ds(4 * half, 4), pl.ds(384 * core, 384)],
            wcs.at[half], wcr.at[half], twin,
        )

    def w_load(j):
        return pltpu.make_async_copy(
            w_ref.at[:, pl.ds(j * WIDTH, WIDTH)], weight.at[col, j], wls.at[j]
        )

    def gelu_part(b):
        def step(n, carry):
            rows = pl.ds(pl.multiple_of(b * 128 + n * 16, 16), 16)
            v = hp_ref[rows, :].astype(F32)
            cdf = 0.5 * (1.0 + lax.erf(v * 0.7071067811865476))
            density = jnp.exp(-0.5 * v * v) * 0.3989422804014327
            slope[rows, :] = cdf + v * density
            act[pl.ds(pl.multiple_of(n * 16, 16), 16), :] = (v * cdf).astype(BF)
            return carry

        lax.fori_loop(0, 8, step, 0)
        act_t[:, b * 128 : (b + 1) * 128] = act[...].T

    def wgrad(j):
        def step(h, carry):
            block = gath[j, pl.ds(2 * h, 2)].reshape(768, WIDTH)
            for m in range(2):
                rows = slice(m * 384, (m + 1) * 384)
                got = jnp.dot(act_t[rows, :], block, preferred_element_type=F32) * scaling
                got = got.astype(BF)
                for t in range(3):
                    dense[6 * j + 3 * h + t, rows, :] = got[:, t * 128 : (t + 1) * 128]
            return carry

        lax.fori_loop(0, 2, step, 0)

    def bwd(j, h):
        for m in range(2):
            block = gath[j, 2 * h + m].reshape(384, WIDTH)
            got = lax.dot_general(
                block, weight[h, j], (((1,), (1,)), ((), ())), preferred_element_type=F32
            )
            acc[m * 384 : (m + 1) * 384, :] += got

    def bwd_both(j):
        lax.fori_loop(0, 2, lambda h, c: (bwd(j, h), c)[1], 0)

    def compact(q):
        def step(n, carry):
            s = q * PER + n
            for i in range(6):
                d = jnp.clip(tables[0, i, s], 0, 47)
                for u in range(4):
                    g = 4 * i + u
                    kept[s, g // 6, (g // 3) % 2, g % 3] = dense[d, g * 32 : (g + 1) * 32, :]
            return carry

        lax.fori_loop(0, PER, step, 0)

    def trade(q):
        some = pl.ds(q * PER, PER)
        return send(kept.at[some, :, 1 - core], summed.at[some], cs.at[q], cr.at[q], twin)

    sign = 1 - 2 * col
    order = (lax.rem(a + 2, 4), lax.rem(a + sign + 4, 4), lax.rem(a - sign + 4, 4), a)
    lands = (land1, land2, land3, land4)

    def hop(q, st):
        some = pl.ds(q * PER, PER)
        return send(
            summed.at[some, order[st]], lands[st].at[some],
            rs.at[q, st], rr.at[q, st], pair if st % 2 else other,
        )

    def sum_cores(q):
        def step(n, carry):
            s = q * PER + n
            summed[s] = (summed[s].astype(F32) + kept[s, :, core].astype(F32)).astype(BF)
            return carry

        lax.fori_loop(0, PER, step, 0)

    def add_land(q, st):
        def step(n, carry):
            s = q * PER + n
            k = order[st + 1]
            summed[s, k] = (summed[s, k].astype(F32) + lands[st][s].astype(F32)).astype(BF)
            return carry

        lax.fori_loop(0, PER, step, 0)

    def add_last(q):
        def step(n, carry):
            s = q * PER + n
            fin[s] = (summed[s, a].astype(F32) + land4[s].astype(F32)).astype(BF)
            return carry

        lax.fori_loop(0, PER, step, 0)

    def event(q, st):
        if st == 0:
            trade(q).wait_recv()
            sum_cores(q)
        else:
            hop(q, st - 1).wait_recv()
            if st == 4:
                add_last(q)
                return
            add_land(q, st - 1)
        hop(q, st).start()

    barrier = pltpu.get_barrier_semaphore()
    for peer in (xp, xm, yp, ym, zp, zm, twin, swap):
        pl.semaphore_signal(barrier, inc=1, device_id=peer, device_id_type=MESH)
    for j in range(CHUNKS):
        w_load(j).start()
    pl.semaphore_wait(barrier, 8)

    start_cross(0)
    place_copy = send(place_ref, place_in, ms, mr, pair)
    place_copy.start()
    start_cross(1)

    @pl.when(jnp.logical_not(crosses))
    def _():
        for j in range(CHUNKS):
            gath[j, y, x] = og_ref[:, j * WIDTH : (j + 1) * WIDTH]

    for j in range(CHUNKS):
        w_load(j).wait()

    def mask_rows(i, carry):
        rows = pl.ds(pl.multiple_of(i * 128, 128), 128)
        for d in range(24):
            lanes = slice((d % 3) * 128, (d % 3 + 1) * 128)
            tile = weight[col, d // 3, rows, lanes]
            keep = jnp.full(tile.shape, mask_ref[i, d], jnp.int32) > 0
            weight[col, d // 3, rows, lanes] = jnp.where(keep, tile.astype(F32), 0.0).astype(BF)
        return carry

    wait_cross(0)
    start(both(first, 0, False))
    lax.fori_loop(0, 6, mask_rows, 0)
    start(w_push(0))
    arrive(both(first, 0, False))
    start(both(first, 0, True))
    gelu_part(0)
    arrive(both(first, 0, True))
    start(both(second, 0, False))
    wait_cross(1)
    start(both(first, 1, False))
    start_cross(2)
    gelu_part(1)
    gelu_part(2)

    place_copy.wait_recv()
    lane = lax.broadcasted_iota(jnp.int32, (8, 128), 1)
    marks = (place_ref[...] + place_in[...]).astype(F32)
    upto = lax.broadcasted_iota(jnp.int32, (128, 128), 0) <= lax.broadcasted_iota(
        jnp.int32, (128, 128), 1
    )
    count = jnp.dot(marks.astype(BF), upto.astype(F32).astype(BF), preferred_element_type=F32)
    places = jnp.zeros((8, 128), F32)
    for s in range(SLOTS):
        before = jnp.where((count < s + 0.5) & (lane < 48), 1.0, 0.0)
        places = jnp.where(lane == s, jnp.sum(before, axis=1, keepdims=True), places)
    table[0] = jnp.minimum(places, 47.0).astype(jnp.int32)
    table[1] = jnp.clip(count - 1.0, 0.0, SLOTS - 1.0).astype(jnp.int32)
    to_scalars = pltpu.make_async_copy(table, tables, tsem)
    to_scalars.start()
    to_scalars.wait()

    acc[...] = jnp.zeros_like(acc)
    for p in range(PAIRS):
        if p < PAIRS - 1:
            arrive(both(first, p + 1, False))
            start(both(first, p + 1, True))
        if p == 0:
            gelu_part(3)
            gelu_part(4)
        else:
            if p % 2 == 1:
                w_relay(p // 2).wait_recv()
            wgrad(2 * p - 2)
            bwd_both(2 * p - 2)
        arrive(both(second, p, False))
        start(both(second, p, True))
        if p < PAIRS - 1:
            arrive(both(first, p + 1, True))
            start(both(second, p + 1, False))
        if p < PAIRS - 2:
            wait_cross(p + 2)
            start(both(first, p + 2, False))
        if p < PAIRS - 3:
            start_cross(p + 3)
        if p == 0:
            gelu_part(5)
        else:
            wgrad(2 * p - 1)
            bwd_both(2 * p - 1)
        if p % 2 == 0:
            arrive(w_push(p // 2))
            w_relay(p // 2).start()
            if p == 0:
                start(w_push(1))
        if p == PAIRS - 1:
            for q in range(EARLY):
                compact(q)
                trade(q).start()
            for q in range(EARLY):
                event(q, 0)
        arrive(both(second, p, True))

    wgrad(2 * PAIRS - 2)
    event(0, 1)
    wgrad(2 * PAIRS - 1)
    event(1, 1)
    for q in range(EARLY, GROUPS):
        compact(q)
        trade(q).start()
    event(0, 2)
    rest = [
        lambda: bwd(2 * PAIRS - 2, 0),
        lambda: bwd(2 * PAIRS - 2, 1),
        lambda: bwd(2 * PAIRS - 1, 0),
        lambda: bwd(2 * PAIRS - 1, 1),
    ]

    def finish():
        def step(n, carry):
            rows = pl.ds(pl.multiple_of(n * 32, 32), 32)
            in_ref[rows, :] = (acc[rows, :] * slope[rows, :]).astype(BF)
            return carry

        lax.fori_loop(0, 24, step, 0)

    rest.append(finish)
    todo = [(2, 0), (3, 0), (1, 2), (0, 3), (2, 1), (3, 1), (1, 3), (0, 4), (2, 2), (3, 2), (1, 4),
            (2, 3), (3, 3), (2, 4), (3, 4)]
    for n, (q, st) in enumerate(todo):
        event(q, st)
        if n >= 1 and rest:
            rest.pop(0)()

    for g in range(3):
        i = (3 * dp + g) // 4
        for d in range(24):
            s = jnp.clip(tables[1, i, 6 * (d // 3) + 3 * col + d % 3], 0, SLOTS - 1)
            tile = fin[s, g]
            keep = jnp.full(tile.shape, mask_ref[i, d], jnp.int32) > 0
            out_ref[g * 32 : (g + 1) * 32, d * 128 : (d + 1) * 128] = jnp.where(
                keep, tile.astype(F32), 0.0
            ).astype(BF)

    @pl.when(crosses)
    def _():
        for j in range(CHUNKS):
            cross(j).wait_send()

    place_copy.wait_send()
    for p in range(PAIRS):
        for f in (False, True):
            left(both(first, p, f))
            left(both(second, p, f))
    for half in range(2):
        left(w_push(half))
        w_relay(half).wait_send()
    for q in range(GROUPS):
        trade(q).wait_send()
        for st in range(4):
            hop(q, st).wait_send()


def body(hidden_pre, out_grad, down_weight, tile_mask):
    col = lax.axis_index("col")
    tokens = out_grad.shape[0] * lax.axis_size("row") * lax.axis_size("dp")
    cut = tile_mask.reshape(6, CHUNKS, 1, 3)
    none = jnp.zeros_like(cut)
    place = jnp.where(
        col == 0, jnp.concatenate([cut, none], axis=2), jnp.concatenate([none, cut], axis=2)
    ).reshape(6, 48)
    place = jnp.pad(place, ((0, 2), (0, 80)))
    vm = pl.BlockSpec(memory_space=pltpu.VMEM)
    dma = pltpu.SemaphoreType.DMA
    return pl.pallas_call(
        functools.partial(kernel, 1.0 / math.sqrt(tokens)),
        out_shape=(
            jax.ShapeDtypeStruct((768, 768), BF),
            jax.ShapeDtypeStruct((96, 3072), BF),
        ),
        in_specs=[vm, vm, pl.BlockSpec(memory_space=pl.ANY), pl.BlockSpec(memory_space=pltpu.SMEM), vm],
        out_specs=(vm, vm),
        scratch_shapes=[
            pltpu.VMEM((CHUNKS, 4, 4, 96, WIDTH), BF),
            pltpu.VMEM((2, CHUNKS, 768, WIDTH), BF),
            pltpu.VMEM((768, 768), BF),
            pltpu.VMEM((128, 768), BF),
            pltpu.VMEM((768, 768), F32),
            pltpu.VMEM((768, 768), F32),
            pltpu.VMEM((48, 768, 128), BF),
            pltpu.VMEM((SLOTS, 4, 2, 3, 32, 128), BF),
            pltpu.VMEM((SLOTS, 4, 3, 32, 128), BF),
            pltpu.VMEM((SLOTS, 3, 32, 128), BF),
            pltpu.VMEM((SLOTS, 3, 32, 128), BF),
            pltpu.VMEM((SLOTS, 3, 32, 128), BF),
            pltpu.VMEM((SLOTS, 3, 32, 128), BF),
            pltpu.VMEM((SLOTS, 3, 32, 128), BF),
            pltpu.VMEM((8, 128), jnp.int32),
            pltpu.VMEM((2, 8, 128), jnp.int32),
            pltpu.SMEM((2, 8, 128), jnp.int32),
            dma((CHUNKS,)), dma((CHUNKS,)),
            dma((CHUNKS, 4)), dma((CHUNKS, 4)),
            dma((CHUNKS, 4)), dma((CHUNKS, 4)),
            dma((CHUNKS,)),
            dma((2, 2)), dma((2, 2)), dma((2,)), dma((2,)),
            dma, dma, dma,
            dma((GROUPS,)), dma((GROUPS,)),
            dma((GROUPS, 4)), dma((GROUPS, 4)),
        ],
        compiler_params=pltpu.CompilerParams(
            collective_id=0, has_side_effects=True, vmem_limit_bytes=60 * 2**20
        ),
        name="mlp_backward",
    )(hidden_pre, out_grad, down_weight, tile_mask, place)


def solution(mesh):
    return jax.shard_map(
        body,
        mesh=mesh,
        in_specs=(
            P(("dp", "col"), "row"),
            P(("dp", "row"), "col"),
            P("row", "col"),
            P("row", "col"),
        ),
        out_specs=(P(("dp", "col"), "row"), P(("row", "dp"), "col")),
        check_vma=False,
    )
```

time: 406 us -> 128 us (0.32)
  waiting for transfers between devices: 320 us -> 0 us
  Pallas kernels: 0 us -> 121 us
  matrix products: 37.4 us -> 0 us
  local copies, waits for them, and re-layouts: 21.1 us -> 4.74 us
  between operations: 13.8 us -> 0.66 us
  starting transfers between devices: 7.54 us -> 0 us
    all_gather x3 -> x0, waiting for transfers between devices: 185 us -> none  [the longest x1 77.6 us: body(): group_grads = lax.all_gather(out_grad, 'row', axis=0, tiled=True)]
    pallas_call x0 -> x1, Pallas kernels: none -> 121 us  [body(): pl.pallas_call(functools.partial(kernel, 1.0 / math.sqrt(tokens)), out_sh...]
    all_to_all x1 -> x0, waiting for transfers between devices: 83.9 us -> none  [body(): lax.all_to_all(group_grads, 'col', split_axis=0, concat_axis=1, tiled=True)]
    reduce_scatter x1 -> x0, waiting for transfers between devices: 49.4 us -> none  [body(): lax.psum_scatter((product * scaling * kept_mask.astype(jnp.float32)).asty...]
    dot_general x2 -> x0, matrix products: 37.4 us -> none  [the longest x1 24.2 us: body(): lax.dot_general(activated, group_grads, (((0,), (0,)), ((), ())), preferr...]
    all_to_all x1 -> x0, local copies, waits for them, and re-layouts: 12.6 us -> none  [body(): lax.all_to_all(group_grads, 'col', split_axis=0, concat_axis=1, tiled=True)]
    all_to_all x1 -> x0, starting transfers between devices: 7.39 us -> none  [body(): lax.all_to_all(group_grads, 'col', split_axis=0, concat_axis=1, tiled=True)]
  transfers between devices with their start and end apart: 5 -> 0, of which waited for: 5 -> 0; matrix products, arithmetic and copies ran while one was open for 15% -> 0% of each run, Pallas kernels for 0% -> 0%
where the time goes in v1:
time: 128 us; the launch traced here: 126 us
  Pallas kernels  121 us (95%)
  local copies, waits for them, and re-layouts  4.74 us (4%)
    pallas_call x1, Pallas kernels, body(): pl.pallas_call(functools.partial(kernel, 1.0 / math.sqrt(tokens)), out_sh...  121 us
    unnamed x4, local copies, waits for them, and re-layouts  3.24 us

profile of v1, /device:TPU:1, one launch (start us, length us, event | category | flops | bytes accessed | tf_op | source)
XLA Modules:
  0.0 126.5 jit_solution(7522448978318199562)
XLA Ops:
  0.6 0.8 reshape.10
  1.4 0.1 reshape.11
  1.6 0.6 pad.6.place_ref
  2.2 121.0 %mlp_backward.1 = (bf16[768,768]{1,0:T(8,128)(2,1)}, bf16[96,3072]{1,0:T(8,128)(2,1)}) custom-call(bf16[768,768]{1,0:T(8,128)(2,1)} %hp_ref.1, bf16[96,3072]{1,0:T(8,128)(2,1)} %og_ref.1, bf16[768,3072]{1,0:T(8,128)(2,1)} %w_ref.1, s32[6,24]{1,0:T(8,128)} %mask_ref.1, s32[8,128]{1,0:T(8,128)} %pad.6.place_ref), custom_call_target="tpu_custom_call" | custom-call | tf_op jit(solution)/shard_map/mlp_backward/pallas_call | solution.py:414
  123.2 0.0 copy-start
  123.2 2.4 %copy.11 = bf16[768,768]{1,0:T(8,128)(2,1)} copy(bf16[768,768]{1,0:T(8,128)(2,1)} %get-tuple-element.4) | data formatting | bytes 2359296
  125.6 0.0 copy-done
  125.6 0.8 copy.12
  (2 shorter events, 0.0 us)
Async XLA Ops:
  123.2 2.4 %copy-start = (bf16[96,3072]{1,0:T(8,128)(2,1)S(1)}, bf16[96,3072]{1,0:T(8,128)(2,1)}, u32[]{:S(2)}) copy-start(bf16[96,3072]{1,0:T(8,128)(2,1)} %get-tuple-element.5) | copy-start | bytes 1769476

commit v2 on v0

v2 whole, which is shorter than its diff:
```python
import functools
import math

import jax
import jax.numpy as jnp
from jax import lax
from jax.experimental import pallas as pl
from jax.experimental.pallas import tpu as pltpu
from jax.sharding import PartitionSpec as P

MESH = pl.DeviceIdType.MESH
BF, F32 = jnp.bfloat16, jnp.float32
TILES = (2, 2, 2, 2, 2, 2)
PAIRS = len(TILES)
STARTS = tuple(2 * sum(TILES[:p]) for p in range(PAIRS))
SLOTS = 24
SIZES = (4, 4, 4, 4, 4, 4)
GROUPS = len(SIZES)
FIRST = tuple(sum(SIZES[:q]) for q in range(GROUPS))


def place_of(d, half):
    p = max(q for q in range(PAIRS) if STARTS[q] <= d)
    c, t = divmod(d - STARTS[p], TILES[p])
    return 2 * STARTS[p] + c * 2 * TILES[p] + half * TILES[p] + t


def kernel(scaling, hp_ref, og_ref, w_ref, mask_ref, in_ref, fin, slots_ref, *scratch):
    gath, weight, staged = (scratch[n * PAIRS : (n + 1) * PAIRS] for n in range(3))
    scratch = scratch[3 * PAIRS :]
    (
        act_t, act, slope, acc, dense, kept, summed, land1, land2, land3, land4,
        place_out, place_in, table, tables,
        p0s, p0r, p1s, p1r, p2s, p2r, wls, wzs, wzr, wcs, wcr, ms, mr, tsem, cs, cr, rs, rr,
    ) = scratch
    dp, row, col = lax.axis_index("dp"), lax.axis_index("row"), lax.axis_index("col")
    x, y, core, a = lax.rem(row, 4), row // 4, lax.rem(dp, 2), dp // 2
    z = a * 2 + col

    def chip(px, py, pz, pc):
        px, py, pz = lax.rem(px + 4, 4), lax.rem(py + 4, 4), lax.rem(pz + 8, 8)
        return ((pz // 2) * 2 + pc, py * 4 + px, lax.rem(pz, 2))

    def slot(py):
        py = lax.rem(py + 4, 4)
        return py + lax.rem(py // 2 + col, 2) * (1 - 2 * lax.rem(py, 2))

    xp, xm = chip(x + 1, y, z, core), chip(x - 1, y, z, core)
    yp, ym = chip(x, y + 1, z, core), chip(x, y - 1, z, core)
    zp, zm = chip(x, y, z + 1, core), chip(x, y, z - 1, core)
    pair = (dp, row, 1 - col)
    other = chip(x, y, z - 1 + 2 * col, core)
    twin = (a * 2 + 1 - core, row, col)
    step_y = 2 * lax.rem(y, 2) - 1
    swap = (dp, lax.rem(y + step_y + 4, 4) * 4 + x, 1 - col)
    crosses = y // 2 != col
    mine, above, below = slot(y), slot(y + 1), slot(y - 1)
    right, left_ = lax.rem(x + 1, 4), lax.rem(x + 3, 4)

    def send(src, dst, s, r, to):
        return pltpu.make_async_remote_copy(
            src_ref=src, dst_ref=dst, send_sem=s, recv_sem=r, device_id=to, device_id_type=MESH
        )

    def same(ref, s, r, to):
        return send(ref, ref, s, r, to)

    def columns(p, c):
        return pl.ds((STARTS[p] + c * TILES[p]) * 128, TILES[p] * 128)

    there = lax.rem(y + step_y + 4, 4)
    there = there + lax.rem(there // 2 + 1 - col, 2) * (1 - 2 * lax.rem(there, 2))

    def cross(p):
        return [
            send(staged[p].at[c], gath[p].at[c, there, x], p0s.at[p, c], p0r.at[p, c], swap)
            for c in range(2)
        ]

    def first(p, forward):
        g = gath[p]
        if forward:
            parts = (
                g.at[0, mine, left_, pl.ds(0, 48)], g.at[0, mine, right, pl.ds(48, 48)],
                g.at[1, below, x, pl.ds(0, 48)], g.at[1, above, x, pl.ds(48, 48)],
            )
        else:
            parts = (g.at[0, mine, x],) * 2 + (g.at[1, mine, x],) * 2
        f = 4 if forward else 0
        ends = (xp, xm, yp, ym)
        return [same(parts[k], p1s.at[p, f + k], p1r.at[p, f + k], ends[k]) for k in range(4)]

    def second(p, forward):
        g = gath[p]
        if forward:
            parts = (
                g.at[0, below, pl.ds(0, 2)], g.at[0, above, pl.ds(2, 2)],
                g.at[1, pl.ds(0, 2), left_], g.at[1, pl.ds(2, 2), right],
            )
        else:
            parts = (g.at[0, mine],) * 2 + (g.at[1, :, x],) * 2
        f = 4 if forward else 0
        ends = (yp, ym, xp, xm)
        return [same(parts[k], p2s.at[p, f + k], p2r.at[p, f + k], ends[k]) for k in range(4)]

    def start(copies):
        for c in copies:
            c.start()

    def arrive(copies):
        for c in copies:
            c.wait_recv()

    def left(copies):
        for c in copies:
            c.wait_send()

    def d1(p):
        @pl.when(crosses)
        def _():
            arrive(cross(p))

        start(first(p, False))

    def f1(p):
        arrive(first(p, False))
        start(first(p, True))

    def d2(p):
        arrive(first(p, True))
        start(second(p, False))

    def f2(p):
        arrive(second(p, False))
        start(second(p, True))

    def done(p):
        arrive(second(p, True))

    def w_push(p):
        return [
            same(
                weight[p].at[col, :, pl.ds(384 * core + 192 * k, 192)],
                wzs.at[p, k], wzr.at[p, k], (zp, zm)[k],
            )
            for k in range(2)
        ]

    def w_relay(p):
        return same(
            weight[p].at[1 - col, :, pl.ds(384 * core, 384)], wcs.at[p], wcr.at[p], twin
        )

    def w_load(p, c):
        return pltpu.make_async_copy(
            w_ref.at[:, columns(p, c)], weight[p].at[col, c], wls.at[p, c]
        )

    def w_mask(p):
        def rows_of(i, carry):
            rows = pl.ds(pl.multiple_of(i * 128, 128), 128)
            for c in range(2):
                for t in range(TILES[p]):
                    lanes = slice(t * 128, (t + 1) * 128)
                    tile = weight[p][col, c, rows, lanes]
                    keep = mask_ref[i, STARTS[p] + c * TILES[p] + t]
                    keep = jnp.full(tile.shape, keep, jnp.int32) > 0
                    weight[p][col, c, rows, lanes] = jnp.where(keep, tile.astype(F32), 0.0).astype(BF)
            return carry

        w_load(p, 0).wait()
        w_load(p, 1).wait()
        lax.fori_loop(0, 6, rows_of, 0)
        start(w_push(p))

    def w_pass(p):
        arrive(w_push(p))
        w_relay(p).start()

    def gelu_part(b):
        def step(n, carry):
            rows = pl.ds(pl.multiple_of(b * 128 + n * 16, 16), 16)
            v = hp_ref[rows, :].astype(F32)
            cdf = 0.5 * (1.0 + lax.erf(v * 0.7071067811865476))
            density = jnp.exp(-0.5 * v * v) * 0.3989422804014327
            slope[rows, :] = cdf + v * density
            act[pl.ds(pl.multiple_of(n * 16, 16), 16), :] = (v * cdf).astype(BF)
            return carry

        lax.fori_loop(0, 8, step, 0)
        act_t[:, b * 128 : (b + 1) * 128] = act[...].T

    def wgrad(p):
        wide = TILES[p] * 128

        def step(n, carry):
            c, h = n // 2, lax.rem(n, 2)
            block = gath[p][c, pl.ds(2 * h, 2)].reshape(768, wide)
            base = 2 * STARTS[p] + c * 2 * TILES[p] + h * TILES[p]
            got = jnp.dot(act_t[...], block, preferred_element_type=F32) * scaling
            got = got.astype(BF)
            for t in range(TILES[p]):
                dense[base + t] = got[:, t * 128 : (t + 1) * 128]
            return carry

        lax.fori_loop(0, 4, step, 0)

    def bwd(p, m):
        wide = TILES[p] * 128
        parts = [(c, h) for h in range(2) for c in range(2)]
        block = jnp.concatenate([gath[p][c, 2 * h + m].reshape(384, wide) for c, h in parts], axis=1)
        columns_of = jnp.concatenate([weight[p][h, c] for c, h in parts], axis=1)
        got = lax.dot_general(
            block, columns_of, (((1,), (1,)), ((), ())), preferred_element_type=F32
        )
        acc[m * 384 : (m + 1) * 384, :] += got

    def compact(q):
        def step(n, carry):
            s = FIRST[q] + n
            for i in range(6):
                d = jnp.clip(tables[i, s], 0, 47)
                for u in range(4):
                    g = 4 * i + u
                    kept[s, g // 6, (g // 3) % 2, g % 3] = dense[d, g * 32 : (g + 1) * 32, :]
            return carry

        lax.fori_loop(0, SIZES[q], step, 0)
        trade(q).start()

    def trade(q):
        some = pl.ds(FIRST[q], SIZES[q])
        return send(kept.at[some, :, 1 - core], summed.at[some], cs.at[q], cr.at[q], twin)

    sign = 1 - 2 * col
    order = (lax.rem(a + 2, 4), lax.rem(a + sign + 4, 4), lax.rem(a - sign + 4, 4), a)
    lands = (land1, land2, land3, land4)

    def hop(q, st):
        some = pl.ds(FIRST[q], SIZES[q])
        return send(
            summed.at[some, order[st]], lands[st].at[some],
            rs.at[q, st], rr.at[q, st], pair if st % 2 else other,
        )

    def event(q, st):
        def step(n, carry):
            s = FIRST[q] + n
            if st == 0:
                summed[s] = (summed[s].astype(F32) + kept[s, :, core].astype(F32)).astype(BF)
            elif st < 4:
                k = order[st]
                summed[s, k] = (summed[s, k].astype(F32) + lands[st - 1][s].astype(F32)).astype(BF)
            else:
                fin[s] = (summed[s, a].astype(F32) + land4[s].astype(F32)).astype(BF)
            return carry

        if st == 0:
            trade(q).wait_recv()
        else:
            hop(q, st - 1).wait_recv()
        lax.fori_loop(0, SIZES[q], step, 0)
        if st < 4:
            hop(q, st).start()

    barrier = pltpu.get_barrier_semaphore()
    for peer in (xp, xm, yp, ym, zp, zm, twin, swap):
        pl.semaphore_signal(barrier, inc=1, device_id=peer, device_id_type=MESH)
    for p in range(PAIRS):
        for c in range(2):
            w_load(p, c).start()
    lane = lax.broadcasted_iota(jnp.int32, (8, 128), 1)
    line = lax.broadcasted_iota(jnp.int32, (8, 128), 0)
    marks = jnp.zeros((8, 128), jnp.int32)
    for d in range(24):
        bits = jnp.zeros((8, 128), jnp.int32)
        for i in range(6):
            bits = jnp.where(line == i, mask_ref[i, d], bits)
        where = place_of(d, 0) + col * (place_of(d, 1) - place_of(d, 0))
        marks = jnp.where(lane == where, bits, marks)
    place_out[...] = marks

    @pl.when(jnp.logical_not(crosses))
    def _():
        for p in range(PAIRS):
            for c in range(2):
                gath[p][c, mine, x] = og_ref[:, columns(p, c)]

    @pl.when(crosses)
    def _():
        for p in range(PAIRS):
            for c in range(2):
                staged[p][c] = og_ref[:, columns(p, c)]

    pl.semaphore_wait(barrier, 8)

    def start_cross(p):
        @pl.when(crosses)
        def _():
            start(cross(p))

    start_cross(0)
    start_cross(1)
    place_copy = send(place_out, place_in, ms, mr, pair)
    place_copy.start()
    w_mask(0)
    d1(0)
    start_cross(2)
    d1(1)
    start_cross(3)
    gelu_part(0)
    w_mask(1)
    f1(0)
    d1(2)
    start_cross(4)
    f1(1)
    d1(3)
    start_cross(5)
    w_mask(2)
    d2(0)
    f1(2)
    gelu_part(1)
    d2(1)
    d1(4)
    d1(5)
    w_mask(3)
    w_mask(4)
    w_mask(5)
    f1(3)
    gelu_part(2)
    gelu_part(3)
    f2(0)
    d2(2)
    w_pass(0)
    f1(4)
    gelu_part(4)
    gelu_part(5)
    acc[...] = jnp.zeros_like(acc)
    place_copy.wait_recv()
    marks = (place_out[...] + place_in[...]).astype(F32)
    upto = lax.broadcasted_iota(jnp.int32, (128, 128), 0) <= lax.broadcasted_iota(
        jnp.int32, (128, 128), 1
    )
    count = jnp.dot(marks.astype(BF), upto.astype(F32).astype(BF), preferred_element_type=F32)
    places = jnp.zeros((8, 128), F32)
    for s in range(SLOTS):
        before = jnp.where((count < s + 0.5) & (lane < 48), 1.0, 0.0)
        places = jnp.where(lane == s, jnp.sum(before, axis=1, keepdims=True), places)
    table[...] = jnp.minimum(places, 47.0).astype(jnp.int32)
    slots_ref[...] = jnp.clip(count - 1.0, 0.0, SLOTS - 1.0).astype(jnp.int32)
    to_scalars = pltpu.make_async_copy(table, tables, tsem)
    to_scalars.start()
    to_scalars.wait()
    f1(5)
    f2(1)
    d2(3)
    done(0)
    wgrad(0)
    w_pass(1)
    f2(2)
    d2(4)
    w_relay(0).wait_recv()
    bwd(0, 0)
    bwd(0, 1)
    done(1)
    wgrad(1)
    w_pass(2)
    f2(3)
    d2(5)
    w_relay(1).wait_recv()
    bwd(1, 0)
    bwd(1, 1)
    done(2)
    wgrad(2)
    w_pass(3)
    w_pass(4)
    w_pass(5)
    f2(4)
    w_relay(2).wait_recv()
    bwd(2, 0)
    bwd(2, 1)
    done(3)
    wgrad(3)
    compact(0)
    compact(1)
    f2(5)
    event(0, 0)
    event(1, 0)
    w_relay(3).wait_recv()
    bwd(3, 0)
    done(4)
    wgrad(4)
    compact(2)
    compact(3)
    event(0, 1)
    event(1, 1)
    event(2, 0)
    event(3, 0)
    bwd(3, 1)
    done(5)
    wgrad(5)
    compact(4)
    compact(5)
    event(0, 2)
    event(1, 2)
    event(2, 1)
    event(3, 1)
    event(4, 0)
    event(5, 0)
    event(0, 3)
    w_relay(4).wait_recv()
    bwd(4, 0)
    event(1, 3)
    event(2, 2)
    event(3, 2)
    event(4, 1)
    event(0, 4)
    event(5, 1)
    event(1, 4)
    bwd(4, 1)
    event(2, 3)
    event(4, 2)
    event(3, 3)
    event(5, 2)
    w_relay(5).wait_recv()
    bwd(5, 0)
    event(2, 4)
    event(4, 3)
    event(3, 4)
    event(5, 3)
    bwd(5, 1)
    event(4, 4)
    def finish(n, carry):
        rows = pl.ds(pl.multiple_of(n * 32, 32), 32)
        in_ref[rows, :] = (acc[rows, :] * slope[rows, :]).astype(BF)
        return carry

    lax.fori_loop(0, 24, finish, 0)
    event(5, 4)


    place_copy.wait_send()
    for p in range(PAIRS):

        @pl.when(crosses)
        def _():
            left(cross(p))

        for f in (False, True):
            left(first(p, f))
            left(second(p, f))
        left(w_push(p))
        w_relay(p).wait_send()
    for q in range(GROUPS):
        trade(q).wait_send()
        for st in range(4):
            hop(q, st).wait_send()


def spread(in_ref, fin, slots_ref, mask_ref, in_out, out_ref):
    in_out[...] = in_ref[...]
    dp, col = lax.axis_index("dp"), lax.axis_index("col")
    for g in range(3):
        i = (3 * dp + g) // 4
        for d in range(24):
            where = place_of(d, 0) + col * (place_of(d, 1) - place_of(d, 0))
            s = jnp.clip(slots_ref[i, where], 0, SLOTS - 1)
            tile = fin[s, g]
            keep = jnp.full(tile.shape, mask_ref[i, d], jnp.int32) > 0
            out_ref[g * 32 : (g + 1) * 32, d * 128 : (d + 1) * 128] = jnp.where(
                keep, tile.astype(F32), 0.0
            ).astype(BF)


def body(hidden_pre, out_grad, down_weight, tile_mask):
    tokens = out_grad.shape[0] * lax.axis_size("row") * lax.axis_size("dp")
    vm, hbm = pl.BlockSpec(memory_space=pltpu.VMEM), pl.BlockSpec(memory_space=pl.ANY)
    smem = pl.BlockSpec(memory_space=pltpu.SMEM)
    dma = pltpu.SemaphoreType.DMA
    wides = [128 * n for n in TILES]
    in_grad, packed, slots = pl.pallas_call(
        functools.partial(kernel, 1.0 / math.sqrt(tokens)),
        out_shape=(
            jax.ShapeDtypeStruct((768, 768), BF),
            jax.ShapeDtypeStruct((SLOTS, 3, 32, 128), BF),
            jax.ShapeDtypeStruct((8, 128), jnp.int32),
        ),
        in_specs=[vm, vm, hbm, smem],
        out_specs=(vm, vm, vm),
        scratch_shapes=[
            *[pltpu.VMEM((2, 4, 4, 96, wide), BF) for wide in wides],
            *[pltpu.VMEM((2, 2, 768, wide), BF) for wide in wides],
            *[pltpu.VMEM((2, 96, wide), BF) for wide in wides],
            pltpu.VMEM((768, 768), BF),
            pltpu.VMEM((128, 768), BF),
            pltpu.VMEM((768, 768), F32),
            pltpu.VMEM((768, 768), F32),
            pltpu.VMEM((48, 768, 128), BF),
            pltpu.VMEM((SLOTS, 4, 2, 3, 32, 128), BF),
            pltpu.VMEM((SLOTS, 4, 3, 32, 128), BF),
            *[pltpu.VMEM((SLOTS, 3, 32, 128), BF)] * 4,
            pltpu.VMEM((8, 128), jnp.int32),
            pltpu.VMEM((8, 128), jnp.int32),
            pltpu.VMEM((8, 128), jnp.int32),
            pltpu.SMEM((8, 128), jnp.int32),
            dma((PAIRS, 2)), dma((PAIRS, 2)),
            dma((PAIRS, 8)), dma((PAIRS, 8)),
            dma((PAIRS, 8)), dma((PAIRS, 8)),
            dma((PAIRS, 2)),
            dma((PAIRS, 2)), dma((PAIRS, 2)), dma((PAIRS,)), dma((PAIRS,)),
            dma, dma, dma,
            dma((GROUPS,)), dma((GROUPS,)),
            dma((GROUPS, 4)), dma((GROUPS, 4)),
        ],
        compiler_params=pltpu.CompilerParams(
            collective_id=0, has_side_effects=True, vmem_limit_bytes=60 * 2**20
        ),
        name="mlp_backward",
    )(hidden_pre, out_grad, down_weight, tile_mask)
    return pl.pallas_call(
        spread,
        out_shape=(
            jax.ShapeDtypeStruct((768, 768), BF),
            jax.ShapeDtypeStruct((96, 3072), BF),
        ),
        in_specs=[vm, vm, smem, smem],
        out_specs=(vm, vm),
        name="spread",
    )(in_grad, packed, slots, tile_mask)


def solution(mesh):
    return jax.shard_map(
        body,
        mesh=mesh,
        in_specs=(
            P(("dp", "col"), "row"),
            P(("dp", "row"), "col"),
            P("row", "col"),
            P("row", "col"),
        ),
        out_specs=(P(("dp", "col"), "row"), P(("row", "dp"), "col")),
        check_vma=False,
    )
```

time: 406 us -> 112 us (0.28)
  waiting for transfers between devices: 320 us -> 0 us
  Pallas kernels: 0 us -> 111 us
  matrix products: 37.4 us -> 0 us
  local copies, waits for them, and re-layouts: 21.1 us -> 0 us
  between operations: 13.8 us -> 0.64 us
  starting transfers between devices: 7.54 us -> 0 us
    all_gather x3 -> x0, waiting for transfers between devices: 185 us -> none  [the longest x1 77.6 us: body(): group_grads = lax.all_gather(out_grad, 'row', axis=0, tiled=True)]
    pallas_call x0 -> x2, Pallas kernels: none -> 111 us  [the longest x1 108 us: body(): pl.pallas_call(functools.partial(kernel, 1.0 / math.sqrt(tokens)), out_sh...]
    all_to_all x1 -> x0, waiting for transfers between devices: 83.9 us -> none  [body(): lax.all_to_all(group_grads, 'col', split_axis=0, concat_axis=1, tiled=True)]
    reduce_scatter x1 -> x0, waiting for transfers between devices: 49.4 us -> none  [body(): lax.psum_scatter((product * scaling * kept_mask.astype(jnp.float32)).asty...]
    dot_general x2 -> x0, matrix products: 37.4 us -> none  [the longest x1 24.2 us: body(): lax.dot_general(activated, group_grads, (((0,), (0,)), ((), ())), preferr...]
    all_to_all x1 -> x0, local copies, waits for them, and re-layouts: 12.6 us -> none  [body(): lax.all_to_all(group_grads, 'col', split_axis=0, concat_axis=1, tiled=True)]
    all_to_all x1 -> x0, starting transfers between devices: 7.39 us -> none  [body(): lax.all_to_all(group_grads, 'col', split_axis=0, concat_axis=1, tiled=True)]
    unnamed x8 -> x0, local copies, waits for them, and re-layouts: 5.6 us -> none
  transfers between devices with their start and end apart: 5 -> 0, of which waited for: 5 -> 0; matrix products, arithmetic and copies ran while one was open for 15% -> 0% of each run, Pallas kernels for 0% -> 0%
where the time goes in v2:
time: 112 us
  Pallas kernels  111 us (99%)
    pallas_call x1, Pallas kernels, body(): pl.pallas_call(functools.partial(kernel, 1.0 / math.sqrt(tokens)), out_sh...  108 us
    pallas_call x1, Pallas kernels, body(): pl.pallas_call(spread, out_shape=(jax.ShapeDtypeStruct((768, 768), BF), j...  2.99 us

profile of v2, /device:TPU:1, one launch (start us, length us, event | category | flops | bytes accessed | tf_op | source)
XLA Modules:
  0.0 112.0 jit_solution(12800716958540059152)
XLA Ops:
  0.6 108.4 %mlp_backward.1 = (bf16[768,768]{1,0:T(8,128)(2,1)}, bf16[24,3,32,128]{3,2,1,0:T(8,128)(2,1)}, s32[8,128]{1,0:T(8,128)}) custom-call(bf16[768,768]{1,0:T(8,128)(2,1)} %hp_ref.1, bf16[96,3072]{1,0:T(8,128)(2,1)} %og_ref.1, bf16[768,3072]{1,0:T(8,128)(2,1)} %w_ref.1, s32[6,24]{1,0:T(8,128)} %mask_ref.3), custom_call_target="tpu_custom_call" | custom-call | tf_op jit(solution)/shard_map/mlp_backward/pallas_call | solution.py:481
  109.0 3.0 %spread.1 = (bf16[768,768]{1,0:T(8,128)(2,1)}, bf16[96,3072]{1,0:T(8,128)(2,1)}) custom-call(bf16[768,768]{1,0:T(8,128)(2,1)} %get-tuple-element.5.in_ref, bf16[24,3,32,128]{3,2,1,0:T(8,128)(2,1)} %get-tuple-element.6.fin, s32[8,128]{1,0:T(8,128)} %get-tuple-element.7.slots_ref, s32[6,24]{1,0:T(8,128)} %mask_ref.3), custom_call_target="tpu_custom_call" | custom-call | tf_op jit(solution)/shard_map/spread/pallas_call | solution.py:520

commit v3 on v2

--- a/solution.py
+++ b/solution.py
@@ -10,11 +10,11 @@
 
 MESH = pl.DeviceIdType.MESH
 BF, F32 = jnp.bfloat16, jnp.float32
-TILES = (2, 2, 2, 2, 2, 2)
+TILES = (2, 3, 2, 2, 2, 1)
 PAIRS = len(TILES)
 STARTS = tuple(2 * sum(TILES[:p]) for p in range(PAIRS))
 SLOTS = 24
-SIZES = (4, 4, 4, 4, 4, 4)
+SIZES = (4, 4, 4, 4, 4, 2, 2)
 GROUPS = len(SIZES)
 FIRST = tuple(sum(SIZES[:q]) for q in range(GROUPS))
 
@@ -25,13 +25,14 @@
     return 2 * STARTS[p] + c * 2 * TILES[p] + half * TILES[p] + t
 
 
-def kernel(scaling, hp_ref, og_ref, w_ref, mask_ref, in_ref, fin, slots_ref, *scratch):
+def kernel(scaling, hp_any, og_ref, w_ref, mask_ref, in_any, fin, slots_ref, *scratch):
     gath, weight, staged = (scratch[n * PAIRS : (n + 1) * PAIRS] for n in range(3))
     scratch = scratch[3 * PAIRS :]
     (
         act_t, act, slope, acc, dense, kept, summed, land1, land2, land3, land4,
         place_out, place_in, table, tables,
         p0s, p0r, p1s, p1r, p2s, p2r, wls, wzs, wzr, wcs, wcr, ms, mr, tsem, cs, cr, rs, rr,
+        hp_ref, in_ref, ogs, hps, ins,
     ) = scratch
     dp, row, col = lax.axis_index("dp"), lax.axis_index("row"), lax.axis_index("col")
     x, y, core, a = lax.rem(row, 4), row // 4, lax.rem(dp, 2), dp // 2
@@ -120,6 +121,11 @@
         def _():
             arrive(cross(p))
 
+        @pl.when(jnp.logical_not(crosses))
+        def _():
+            for c in range(2):
+                own(p, c).wait()
+
         start(first(p, False))
 
     def f1(p):
@@ -266,9 +272,30 @@
     barrier = pltpu.get_barrier_semaphore()
     for peer in (xp, xm, yp, ym, zp, zm, twin, swap):
         pl.semaphore_signal(barrier, inc=1, device_id=peer, device_id_type=MESH)
+    def own(p, c):
+        return pltpu.make_async_copy(og_ref.at[:, columns(p, c)], gath[p].at[c, mine, x], ogs.at[p, c])
+
+    def stage(p, c):
+        return pltpu.make_async_copy(og_ref.at[:, columns(p, c)], staged[p].at[c], ogs.at[p, c])
+
+    @pl.when(jnp.logical_not(crosses))
+    def _():
+        for p in range(PAIRS):
+            for c in range(2):
+                own(p, c).start()
+
+    @pl.when(crosses)
+    def _():
+        for p in range(PAIRS):
+            for c in range(2):
+                stage(p, c).start()
+
+    hp_load = pltpu.make_async_copy(hp_any, hp_ref, hps)
     for p in range(PAIRS):
         for c in range(2):
             w_load(p, c).start()
+        if p == 0:
+            hp_load.start()
     lane = lax.broadcasted_iota(jnp.int32, (8, 128), 1)
     line = lax.broadcasted_iota(jnp.int32, (8, 128), 0)
     marks = jnp.zeros((8, 128), jnp.int32)
@@ -280,34 +307,25 @@
         marks = jnp.where(lane == where, bits, marks)
     place_out[...] = marks
 
-    @pl.when(jnp.logical_not(crosses))
-    def _():
-        for p in range(PAIRS):
-            for c in range(2):
-                gath[p][c, mine, x] = og_ref[:, columns(p, c)]
-
-    @pl.when(crosses)
-    def _():
-        for p in range(PAIRS):
-            for c in range(2):
-                staged[p][c] = og_ref[:, columns(p, c)]
-
     pl.semaphore_wait(barrier, 8)
 
     def start_cross(p):
         @pl.when(crosses)
         def _():
+            for c in range(2):
+                stage(p, c).wait()
             start(cross(p))
 
     start_cross(0)
     start_cross(1)
     place_copy = send(place_out, place_in, ms, mr, pair)
     place_copy.start()
+    d1(0)
     w_mask(0)
-    d1(0)
     start_cross(2)
     d1(1)
     start_cross(3)
+    hp_load.wait()
     gelu_part(0)
     w_mask(1)
     f1(0)
@@ -369,66 +387,71 @@
     d2(5)
     w_relay(1).wait_recv()
     bwd(1, 0)
-    bwd(1, 1)
     done(2)
     wgrad(2)
+    compact(0)
     w_pass(3)
-    w_pass(4)
-    w_pass(5)
-    f2(4)
+    bwd(1, 1)
+    event(0, 0)
     w_relay(2).wait_recv()
     bwd(2, 0)
     bwd(2, 1)
+    f2(4)
     done(3)
     wgrad(3)
-    compact(0)
     compact(1)
+    compact(2)
+    event(0, 1)
+    w_pass(4)
+    w_pass(5)
+    event(1, 0)
+    event(2, 0)
     f2(5)
-    event(0, 0)
-    event(1, 0)
+    event(0, 2)
+    done(4)
+    wgrad(4)
+    compact(3)
+    compact(4)
+    event(1, 1)
+    event(2, 1)
+    event(3, 0)
+    done(5)
+    wgrad(5)
+    compact(5)
+    compact(6)
+    event(4, 0)
+    event(0, 3)
+    event(1, 2)
+    event(5, 0)
+    event(6, 0)
+    event(3, 1)
+    event(2, 2)
     w_relay(3).wait_recv()
     bwd(3, 0)
-    done(4)
-    wgrad(4)
-    compact(2)
-    compact(3)
-    event(0, 1)
-    event(1, 1)
-    event(2, 0)
-    event(3, 0)
+    event(4, 1)
+    event(0, 4)
     bwd(3, 1)
-    done(5)
-    wgrad(5)
-    compact(4)
-    compact(5)
-    event(0, 2)
-    event(1, 2)
-    event(2, 1)
-    event(3, 1)
-    event(4, 0)
-    event(5, 0)
-    event(0, 3)
+    event(1, 3)
+    event(3, 2)
+    event(5, 1)
+    event(6, 1)
+    event(4, 2)
     w_relay(4).wait_recv()
     bwd(4, 0)
-    event(1, 3)
-    event(2, 2)
-    event(3, 2)
-    event(4, 1)
-    event(0, 4)
-    event(5, 1)
+    event(2, 3)
     event(1, 4)
+    event(5, 2)
+    event(3, 3)
+    event(6, 2)
     bwd(4, 1)
-    event(2, 3)
-    event(4, 2)
-    event(3, 3)
-    event(5, 2)
+    event(4, 3)
+    event(2, 4)
     w_relay(5).wait_recv()
     bwd(5, 0)
-    event(2, 4)
-    event(4, 3)
+    event(5, 3)
+    event(6, 3)
+    bwd(5, 1)
     event(3, 4)
-    event(5, 3)
-    bwd(5, 1)
     event(4, 4)
     def finish(n, carry):
         rows = pl.ds(pl.multiple_of(n * 32, 32), 32)
@@ -436,9 +459,13 @@
         return carry
 
     lax.fori_loop(0, 24, finish, 0)
+    in_store = pltpu.make_async_copy(in_ref, in_any, ins)
+    in_store.start()
     event(5, 4)
-
-
+    event(6, 4)
+
+
+    in_store.wait()
     place_copy.wait_send()
     for p in range(PAIRS):
 
@@ -485,8 +512,8 @@
             jax.ShapeDtypeStruct((SLOTS, 3, 32, 128), BF),
             jax.ShapeDtypeStruct((8, 128), jnp.int32),
         ),
-        in_specs=[vm, vm, hbm, smem],
-        out_specs=(vm, vm, vm),
+        in_specs=[hbm, hbm, hbm, smem],
+        out_specs=(hbm, vm, vm),
         scratch_shapes=[
             *[pltpu.VMEM((2, 4, 4, 96, wide), BF) for wide in wides],
             *[pltpu.VMEM((2, 2, 768, wide), BF) for wide in wides],
@@ -511,6 +538,9 @@
             dma, dma, dma,
             dma((GROUPS,)), dma((GROUPS,)),
             dma((GROUPS, 4)), dma((GROUPS, 4)),
+            pltpu.VMEM((768, 768), BF),
+            pltpu.VMEM((768, 768), BF),
+            dma((PAIRS, 2)), dma, dma,
         ],
         compiler_params=pltpu.CompilerParams(
             collective_id=0, has_side_effects=True, vmem_limit_bytes=60 * 2**20

time: 112 us -> 109 us (0.973)
  Pallas kernels: 111 us -> 108 us
    pallas_call x1, Pallas kernels: 108 us -> 106 us  [body(): pl.pallas_call(functools.partial(kernel, 1.0 / math.sqrt(tokens)), out_sh...]
where the time goes in v3:
time: 109 us
  Pallas kernels  108 us (99%)
    pallas_call x1, Pallas kernels, body(): pl.pallas_call(functools.partial(kernel, 1.0 / math.sqrt(tokens)), out_sh...  106 us
    pallas_call x1, Pallas kernels, body(): pl.pallas_call(spread, out_shape=(jax.ShapeDtypeStruct((768, 768), BF), j...  2.99 us

profile of v3, /device:TPU:1, one launch (start us, length us, event | category | flops | bytes accessed | tf_op | source)
XLA Modules:
  0.0 109.1 jit_solution(5119616072855181546)
XLA Ops:
  0.6 105.5 %mlp_backward.1 = (bf16[768,768]{1,0:T(8,128)(2,1)}, bf16[24,3,32,128]{3,2,1,0:T(8,128)(2,1)}, s32[8,128]{1,0:T(8,128)}) custom-call(bf16[768,768]{1,0:T(8,128)(2,1)} %hp_any.1, bf16[96,3072]{1,0:T(8,128)(2,1)} %og_ref.1, bf16[768,3072]{1,0:T(8,128)(2,1)} %w_ref.1, s32[6,24]{1,0:T(8,128)} %mask_ref.3), custom_call_target="tpu_custom_call" | custom-call | tf_op jit(solution)/shard_map/mlp_backward/pallas_call | solution.py:508
  106.1 3.0 %spread.1 = (bf16[768,768]{1,0:T(8,128)(2,1)}, bf16[96,3072]{1,0:T(8,128)(2,1)}) custom-call(bf16[768,768]{1,0:T(8,128)(2,1)} %get-tuple-element.5.in_ref, bf16[24,3,32,128]{3,2,1,0:T(8,128)(2,1)} %get-tuple-element.6.fin, s32[8,128]{1,0:T(8,128)} %get-tuple-element.7.slots_ref, s32[6,24]{1,0:T(8,128)} %mask_ref.3), custom_call_target="tpu_custom_call" | custom-call | tf_op jit(solution)/shard_map/spread/pallas_call | solution.py:550

commit v4 on v3

--- a/solution.py
+++ b/solution.py
@@ -268,6 +268,22 @@
         lax.fori_loop(0, SIZES[q], step, 0)
         if st < 4:
             hop(q, st).start()
+
+    def sent_pair(p):
+        @pl.when(crosses)
+        def _():
+            left(cross(p))
+
+        for f in (False, True):
+            left(first(p, f))
+            left(second(p, f))
+        left(w_push(p))
+        w_relay(p).wait_send()
+
+    def sent_group(q):
+        trade(q).wait_send()
+        for st in range(4):
+            hop(q, st).wait_send()
 
     barrier = pltpu.get_barrier_semaphore()
     for peer in (xp, xm, yp, ym, zp, zm, twin, swap):
@@ -321,35 +337,34 @@
     place_copy = send(place_out, place_in, ms, mr, pair)
     place_copy.start()
     d1(0)
-    w_mask(0)
     start_cross(2)
     d1(1)
     start_cross(3)
     hp_load.wait()
     gelu_part(0)
-    w_mask(1)
     f1(0)
     d1(2)
     start_cross(4)
     f1(1)
     d1(3)
     start_cross(5)
-    w_mask(2)
     d2(0)
     f1(2)
     gelu_part(1)
     d2(1)
     d1(4)
+    w_mask(0)
     d1(5)
+    w_mask(1)
+    w_mask(2)
+    f1(3)
+    gelu_part(2)
     w_mask(3)
+    gelu_part(3)
     w_mask(4)
     w_mask(5)
-    f1(3)
-    gelu_part(2)
-    gelu_part(3)
     f2(0)
     d2(2)
-    w_pass(0)
     f1(4)
     gelu_part(4)
     gelu_part(5)
@@ -374,6 +389,7 @@
     d2(3)
     done(0)
     wgrad(0)
+    w_pass(0)
     w_pass(1)
     f2(2)
     d2(4)
@@ -426,8 +442,10 @@
     event(6, 0)
     event(3, 1)
     event(2, 2)
+    sent_pair(0)
     w_relay(3).wait_recv()
     bwd(3, 0)
+    sent_pair(1)
     event(4, 1)
     event(0, 4)
     bwd(3, 1)
@@ -436,23 +454,31 @@
     event(5, 1)
     event(6, 1)
     event(4, 2)
+    sent_pair(2)
     w_relay(4).wait_recv()
     bwd(4, 0)
+    sent_pair(3)
     event(2, 3)
     event(1, 4)
     event(5, 2)
     event(3, 3)
     event(6, 2)
+    sent_pair(4)
     bwd(4, 1)
     event(4, 3)
     event(2, 4)
+    sent_pair(5)
     w_relay(5).wait_recv()
     bwd(5, 0)
     event(5, 3)
     event(6, 3)
+    sent_group(0)
+    sent_group(1)
     bwd(5, 1)
     event(3, 4)
+    sent_group(2)
     event(4, 4)
+    sent_group(3)
     def finish(n, carry):
         rows = pl.ds(pl.multiple_of(n * 32, 32), 32)
         in_ref[rows, :] = (acc[rows, :] * slope[rows, :]).astype(BF)
@@ -461,27 +487,15 @@
     lax.fori_loop(0, 24, finish, 0)
     in_store = pltpu.make_async_copy(in_ref, in_any, ins)
     in_store.start()
+    sent_group(4)
     event(5, 4)
     event(6, 4)
 
 
     in_store.wait()
     place_copy.wait_send()
-    for p in range(PAIRS):
-
-        @pl.when(crosses)
-        def _():
-            left(cross(p))
-
-        for f in (False, True):
-            left(first(p, f))
-            left(second(p, f))
-        left(w_push(p))
-        w_relay(p).wait_send()
-    for q in range(GROUPS):
-        trade(q).wait_send()
-        for st in range(4):
-            hop(q, st).wait_send()
+    sent_group(5)
+    sent_group(6)
 
 
 def spread(in_ref, fin, slots_ref, mask_ref, in_out, out_ref):

time: 109 us -> 108 us (level)
    pallas_call x1, Pallas kernels: 106 us -> 104 us  [body(): pl.pallas_call(functools.partial(kernel, 1.0 / math.sqrt(tokens)), out_sh...]
where the time goes in v4:
time: 108 us; the launch traced here: 107 us
  Pallas kernels  107 us (99%)
    pallas_call x1, Pallas kernels, body(): pl.pallas_call(functools.partial(kernel, 1.0 / math.sqrt(tokens)), out_sh...  104 us
    pallas_call x1, Pallas kernels, body(): pl.pallas_call(spread, out_shape=(jax.ShapeDtypeStruct((768, 768), BF), j...  2.99 us

profile of v4, /device:TPU:1, one launch (start us, length us, event | category | flops | bytes accessed | tf_op | source)
XLA Modules:
  0.0 107.4 jit_solution(7472618514633862148)
XLA Ops:
  0.6 103.8 %mlp_backward.1 = (bf16[768,768]{1,0:T(8,128)(2,1)}, bf16[24,3,32,128]{3,2,1,0:T(8,128)(2,1)}, s32[8,128]{1,0:T(8,128)}) custom-call(bf16[768,768]{1,0:T(8,128)(2,1)} %hp_any.1, bf16[96,3072]{1,0:T(8,128)(2,1)} %og_ref.1, bf16[768,3072]{1,0:T(8,128)(2,1)} %w_ref.1, s32[6,24]{1,0:T(8,128)} %mask_ref.3), custom_call_target="tpu_custom_call" | custom-call | tf_op jit(solution)/shard_map/mlp_backward/pallas_call | solution.py:522
  104.4 3.0 %spread.1 = (bf16[768,768]{1,0:T(8,128)(2,1)}, bf16[96,3072]{1,0:T(8,128)(2,1)}) custom-call(bf16[768,768]{1,0:T(8,128)(2,1)} %get-tuple-element.5.in_ref, bf16[24,3,32,128]{3,2,1,0:T(8,128)(2,1)} %get-tuple-element.6.fin, s32[8,128]{1,0:T(8,128)} %get-tuple-element.7.slots_ref, s32[6,24]{1,0:T(8,128)} %mask_ref.3), custom_call_target="tpu_custom_call" | custom-call | tf_op jit(solution)/shard_map/spread/pallas_call | solution.py:564

commit v5 on v4

--- a/solution.py
+++ b/solution.py
@@ -306,6 +306,17 @@
             for c in range(2):
                 stage(p, c).start()
 
+    pl.semaphore_wait(barrier, 8)
+
+    def start_cross(p):
+        @pl.when(crosses)
+        def _():
+            for c in range(2):
+                stage(p, c).wait()
+            start(cross(p))
+
+    start_cross(0)
+    start_cross(1)
     hp_load = pltpu.make_async_copy(hp_any, hp_ref, hps)
     for p in range(PAIRS):
         for c in range(2):
@@ -323,17 +334,6 @@
         marks = jnp.where(lane == where, bits, marks)
     place_out[...] = marks
 
-    pl.semaphore_wait(barrier, 8)
-
-    def start_cross(p):
-        @pl.when(crosses)
-        def _():
-            for c in range(2):
-                stage(p, c).wait()
-            start(cross(p))
-
-    start_cross(0)
-    start_cross(1)
     place_copy = send(place_out, place_in, ms, mr, pair)
     place_copy.start()
     d1(0)

time: 108 us -> 108 us (level)
  no operation moved by 1% of the time
where the time goes in v5:
time: 108 us
  Pallas kernels  107 us (99%)
    pallas_call x1, Pallas kernels, body(): pl.pallas_call(functools.partial(kernel, 1.0 / math.sqrt(tokens)), out_sh...  104 us
    pallas_call x1, Pallas kernels, body(): pl.pallas_call(spread, out_shape=(jax.ShapeDtypeStruct((768, 768), BF), j...  2.99 us

profile of v5, /device:TPU:1, one launch (start us, length us, event | category | flops | bytes accessed | tf_op | source)
XLA Modules:
  0.0 107.7 jit_solution(12613921903076132282)
XLA Ops:
  0.6 104.1 %mlp_backward.1 = (bf16[768,768]{1,0:T(8,128)(2,1)}, bf16[24,3,32,128]{3,2,1,0:T(8,128)(2,1)}, s32[8,128]{1,0:T(8,128)}) custom-call(bf16[768,768]{1,0:T(8,128)(2,1)} %hp_any.1, bf16[96,3072]{1,0:T(8,128)(2,1)} %og_ref.1, bf16[768,3072]{1,0:T(8,128)(2,1)} %w_ref.1, s32[6,24]{1,0:T(8,128)} %mask_ref.3), custom_call_target="tpu_custom_call" | custom-call | tf_op jit(solution)/shard_map/mlp_backward/pallas_call | solution.py:522
  104.7 3.0 %spread.1 = (bf16[768,768]{1,0:T(8,128)(2,1)}, bf16[96,3072]{1,0:T(8,128)(2,1)}) custom-call(bf16[768,768]{1,0:T(8,128)(2,1)} %get-tuple-element.5.in_ref, bf16[24,3,32,128]{3,2,1,0:T(8,128)(2,1)} %get-tuple-element.6.fin, s32[8,128]{1,0:T(8,128)} %get-tuple-element.7.slots_ref, s32[6,24]{1,0:T(8,128)} %mask_ref.3), custom_call_target="tpu_custom_call" | custom-call | tf_op jit(solution)/shard_map/spread/pallas_call | solution.py:564
